TPU v7x, 1024 devices: a whole 4x8x16 slice. The times are simulated.
1024 devices in a mesh: node: 64 (over x, y, core), local: 16 (over z).
Axes of the slice: x: 4, y: 8, z: 16, core: 2. Of those that a mesh axis runs over, the one named last changes fastest.
Arguments:
- tokens: bfloat16 [2048, 3584], P('node', 'local'), may hold values from -6 to 6
- grad_out: bfloat16 [2048, 3584], P('node', 'local'), may hold values from -6 to 6
- route_prob: bfloat16 [2048, 4], P('node'), may hold values from 0.049804688 to 0.59765625
- route_expert: int32 [2048, 4], P('node'), may hold values from 0 to 63, all different within a row; in each aligned block of 32 rows (0 to 31, 32 to 63, ...) at most 4 rows name the same one
- w_gate: bfloat16 [64, 3584, 2048], P('node', 'local'), may hold values from -0.125 to 0.125
- w_up: bfloat16 [64, 3584, 2048], P('node', 'local'), may hold values from -0.125 to 0.125
- w_down: bfloat16 [64, 2048, 3584], P('node', None, 'local'), may hold values from -0.09375 to 0.09375
Outputs:
- grad_tokens: bfloat16 [2048, 3584], P('node', 'local')
- grad_prob: bfloat16 [2048, 4], P('node')
Inputs may be any that keep to these rules, and one draw needn't show every extreme that they name: `route_expert`: each row names 4 different experts; in each block of 32 rows no expert is named by more than 4 rows, a bound that some block reaches.
All inputs are finite; a program needn't handle non-finite values.
Results may differ from a plain program's by a relative error of at most 0.022.
Values may be sent and summed in bfloat16 or wider, within the bound.
A program may use at most 32 MiB of HBM per device.

v0:
```python
import jax
import jax.numpy as jnp
from jax import lax
from jax.sharding import PartitionSpec as P

CAP = 4


def route_slots(block_routes, experts, capacity):
    flat_ids = block_routes.reshape(-1)
    onehot = (flat_ids[:, None] == jnp.arange(experts, dtype=jnp.int32)[None, :]).astype(jnp.int32)
    earlier = jnp.cumsum(onehot, axis=0) - onehot
    ranked = jnp.sum(earlier * onehot, axis=1)
    return flat_ids * capacity + ranked


def swiglu_back(gate_sum, up_sum, back_sum, weights):
    squash = jax.nn.sigmoid(gate_sum)
    gated_act = gate_sum * squash
    grad_hidden = back_sum * weights.astype(jnp.float32)[:, None]
    grad_up = (grad_hidden * gated_act).astype(jnp.bfloat16)
    grad_gate = (grad_hidden * up_sum * squash * (1.0 + gate_sum * (1.0 - squash))).astype(
        jnp.bfloat16
    )
    prob_part = jnp.sum(gated_act * up_sum * back_sum, axis=1)
    return (grad_gate, grad_up, prob_part)


def on_device(tokens, grad_out, route_prob, route_expert, w_gate, w_up, w_down):
    node_count = lax.axis_size("node")
    node_tokens, top_count = route_expert.shape
    columns = tokens.shape[1]
    capacity = CAP
    slot_total = node_count * capacity
    positions = route_slots(route_expert, node_count, capacity)
    route_count = node_tokens * top_count
    source_row = (
        jnp.full((slot_total,), node_tokens, jnp.int32)
        .at[positions]
        .set(jnp.arange(route_count, dtype=jnp.int32) // top_count)
    )
    send_prob = jnp.zeros((slot_total,), jnp.bfloat16).at[positions].set(route_prob.reshape(-1))
    padded_tokens = jnp.concatenate([tokens, jnp.zeros((1, columns), tokens.dtype)], axis=0)
    padded_grads = jnp.concatenate([grad_out, jnp.zeros((1, columns), grad_out.dtype)], axis=0)
    send_rows = padded_tokens[source_row].reshape(node_count, capacity, columns)
    send_grads = padded_grads[source_row].reshape(node_count, capacity, columns)
    arrived_rows, arrived_grads, arrived_prob = (
        lax.all_to_all(send_rows, "node", split_axis=0, concat_axis=0, tiled=True),
        lax.all_to_all(send_grads, "node", split_axis=0, concat_axis=0, tiled=True),
        lax.all_to_all(
            send_prob.reshape(node_count, capacity), "node", split_axis=0, concat_axis=0, tiled=True
        ),
    )
    slot_rows = arrived_rows.reshape(slot_total, columns)
    slot_grads = arrived_grads.reshape(slot_total, columns)
    slot_prob = arrived_prob.reshape(slot_total)
    gate_weight = w_gate[0]
    up_weight = w_up[0]
    down_weight = w_down[0]
    gate_part = jnp.dot(slot_rows, gate_weight, preferred_element_type=jnp.float32)
    up_part = jnp.dot(slot_rows, up_weight, preferred_element_type=jnp.float32)
    back_part = lax.dot_general(
        slot_grads, down_weight, (((1,), (1,)), ((), ())), preferred_element_type=jnp.float32
    )
    gate_sum, up_sum, back_sum = (
        lax.psum_scatter(gate_part, "local", scatter_dimension=1, tiled=True),
        lax.psum_scatter(up_part, "local", scatter_dimension=1, tiled=True),
        lax.psum_scatter(back_part, "local", scatter_dimension=1, tiled=True),
    )
    grad_gate, grad_up, prob_part = swiglu_back(gate_sum, up_sum, back_sum, slot_prob)
    prob_grad = lax.psum(prob_part, "local").astype(jnp.bfloat16)
    running = lax.dot_general(
        lax.all_gather(grad_gate, "local", axis=1, tiled=True),
        gate_weight,
        (((1,), (1,)), ((), ())),
        preferred_element_type=jnp.float32,
    )
    slot_dx = running + lax.dot_general(
        lax.all_gather(grad_up, "local", axis=1, tiled=True),
        up_weight,
        (((1,), (1,)), ((), ())),
        preferred_element_type=jnp.float32,
    )
    returned_dx, returned_prob = (
        lax.all_to_all(
            slot_dx.astype(jnp.bfloat16).reshape(node_count, capacity, columns),
            "node",
            split_axis=0,
            concat_axis=0,
            tiled=True,
        ),
        lax.all_to_all(
            prob_grad.reshape(node_count, capacity), "node", split_axis=0, concat_axis=0, tiled=True
        ),
    )
    picked = returned_dx.reshape(slot_total, columns)[positions].astype(jnp.float32)
    grad_tokens = jnp.sum(picked.reshape(node_tokens, top_count, columns), axis=1).astype(
        jnp.bfloat16
    )
    grad_prob = returned_prob.reshape(slot_total)[positions].reshape(node_tokens, top_count)
    return (grad_tokens, grad_prob)


def solution(mesh):
    return jax.shard_map(
        on_device,
        mesh=mesh,
        in_specs=(
            P("node", "local"),
            P("node", "local"),
            P("node", None),
            P("node", None),
            P("node", "local", None),
            P("node", "local", None),
            P("node", None, "local"),
        ),
        out_specs=(P("node", "local"), P("node", None)),
        check_vma=False,
    )
```

profile of v0, /device:TPU:1, one launch (start us, length us, event | category | flops | bytes accessed | tf_op | source)
XLA Modules:
  0.0 452.0 jit_solution(134141886066844966)
XLA Ops:
  7.2 0.9 copy.20
  8.1 0.7 broadcast_multiply_fusion
  9.6 1.0 scatter_custom_fusion
  10.6 0.7 concatenate.7
  11.3 1.1 gather_fusion.1
  12.5 27.9 %all_to_all.35 = bf16[64,4,224]{2,1,0:T(4,128)(2,1)S(1)} all-to-all(bf16[64,4,224]{2,1,0:T(4,128)(2,1)S(1)} %reshape.84), channel_id=1, replica_groups=mesh['node'=64,'local'=16] {'node'}, dimensions={0} | all-to-all | bytes 229376 | tf_op jit(solution)/shard_map/all_to_all | solution.py:48
  40.5 1.8 fusion.6
  42.4 1.7 fusion.3
  44.2 1.2 gather_fusion
  45.4 15.0 %all_to_all.36 = bf16[64,4,224]{2,1,0:T(4,128)(2,1)S(1)} all-to-all(bf16[64,4,224]{2,1,0:T(4,128)(2,1)S(1)} %reshape.81), channel_id=1, replica_groups=mesh['node'=64,'local'=16] {'node'}, dimensions={0} | all-to-all | bytes 229376 | tf_op jit(solution)/shard_map/all_to_all | solution.py:49
  60.5 1.8 fusion.8
  62.6 1.3 scatter_custom_fusion.1
  64.1 14.0 %all_to_all.37 = bf16[64,1,4]{2,1,0:T(2,128)(2,1)S(1)} all-to-all(bf16[64,1,4]{2,1,0:T(2,128)(2,1)S(1)} %all_to_all.28), channel_id=1, replica_groups=mesh['node'=64,'local'=16] {'node'}, dimensions={0} | all-to-all | bytes 1024 | tf_op jit(solution)/shard_map/all_to_all | solution.py:50
  78.2 27.2 %reduce-scatter.6.cloned.1.call-done = f32[256,128]{1,0:T(8,128)} async-done(((f32[256,2048]{1,0:T(8,128)}), f32[256,128]{1,0:T(8,128)}) %reduce-scatter.6.cloned.1.call-update) | async-done | bytes 131088 | tf_op jit(solution)/shard_map/reduce_scatter | solution.py:67
  105.5 77.2 %reduce-scatter.8.cloned.1.call-done = f32[256,128]{1,0:T(8,128)} async-done(((f32[256,2048]{1,0:T(8,128)}), f32[256,128]{1,0:T(8,128)}) %reduce-scatter.8.cloned.1.call-update) | async-done | bytes 131088 | tf_op jit(solution)/shard_map/reduce_scatter | solution.py:66
  182.7 77.7 %reduce-scatter.4.cloned.1.call-done = f32[256,128]{1,0:T(8,128)} async-done(((f32[256,2048]{1,0:T(8,128)}), f32[256,128]{1,0:T(8,128)}) %reduce-scatter.4.cloned.1.call-update) | async-done | bytes 131088 | tf_op jit(solution)/shard_map/reduce_scatter | solution.py:68
  260.3 1.9 multiply_reduce_fusion
  262.3 0.5 all-gather.5.cloned.1.call-update
  262.8 22.1 %psum.7 = bf16[256]{0:T(256)(128)(2,1)S(1)} all-reduce(f32[256]{0:T(256)S(1)} %get-tuple-element.8), channel_id=1, replica_groups=mesh['node'=64,'local'=16] {'local'}, use_global_device_ids=true, to_apply=%region_9.10 | all-reduce | flops 256 | bytes 1536 | tf_op jit(solution)/shard_map/psum | solution.py:71
  285.0 0.7 all_to_all.29
  285.7 26.9 %all-to-all-start.4 = ((bf16[64,1,4]{2,1,0:T(2,128)(2,1)}), bf16[64,1,4]{2,1,0:T(2,128)(2,1)S(1)}, u32[]{:S(2)}, u32[]{:S(2)}) async-start(bf16[64,1,4]{2,1,0:T(2,128)(2,1)} %all_to_all.29), calls=%async_computation.7 | async-start | bytes 65536 | tf_op jit(solution)/shard_map/all_to_all | solution.py:92
  312.6 23.8 %all-gather.3.cloned.1.call-done = bf16[256,2048]{1,0:T(8,128)(2,1)} async-done(((bf16[256,128]{1,0:T(8,128)(2,1)}), bf16[256,2048]{1,0:T(8,128)(2,1)}) %all-gather.3.cloned.1.call-update) | async-done | bytes 1048592 | tf_op jit(solution)/shard_map/all_gather | solution.py:73
  336.5 1.7 fusion.1
  338.2 71.7 %all-gather.5.cloned.1.call-done = bf16[256,2048]{1,0:T(8,128)(2,1)} async-done(((bf16[256,128]{1,0:T(8,128)(2,1)}), bf16[256,2048]{1,0:T(8,128)(2,1)}) %all-gather.5.cloned.1.call-update) | async-done | bytes 1048592 | tf_op jit(solution)/shard_map/all_gather | solution.py:79
  409.9 1.7 fusion
  411.7 0.7 reshape.86
  412.4 21.1 %all-to-all-start.3 = ((bf16[64,4,224]{2,1,0:T(4,128)(2,1)}), bf16[64,4,224]{2,1,0:T(4,128)(2,1)S(1)}, u32[]{:S(2)}, u32[]{:S(2)}) async-start(bf16[64,4,224]{2,1,0:T(4,128)(2,1)} %reshape.86), calls=%async_computation.6 | async-start | bytes 262144 | tf_op jit(solution)/shard_map/all_to_all | solution.py:85
  433.7 1.2 gather_fusion.3
  435.1 0.7 copy.25
  435.7 8.1 %all-to-all-done.3 = bf16[64,4,224]{2,1,0:T(4,128)(2,1)S(1)} async-done(((bf16[64,4,224]{2,1,0:T(4,128)(2,1)}), bf16[64,4,224]{2,1,0:T(4,128)(2,1)S(1)}, u32[]{:S(2)}, u32[]{:S(2)}) %all-to-all-start.3) | async-done | bytes 114720 | tf_op jit(solution)/shard_map/all_to_all | solution.py:85
  443.9 0.8 gather_fusion.2
  444.8 0.7 reduce_sum.34
  (47 shorter events, 2.4 us)
Async XLA Ops:
  7.2 35.2 %copy-start = (bf16[1,224,2048]{2,1,0:T(8,128)(2,1)S(1)}, bf16[1,224,2048]{2,1,0:T(8,128)(2,1)}, u32[]{:S(2)}) copy-start(bf16[1,224,2048]{2,1,0:T(8,128)(2,1)} %param.11) | copy-start | bytes 2752516
  7.2 33.3 %copy-start.1 = (bf16[1,224,2048]{2,1,0:T(8,128)(2,1)S(1)}, bf16[1,224,2048]{2,1,0:T(8,128)(2,1)}, u32[]{:S(2)}) copy-start(bf16[1,224,2048]{2,1,0:T(8,128)(2,1)} %param.12) | copy-start | bytes 2752516
  7.2 98.3 %reduce-scatter.6.cloned.1.call-start = ((), (), s32[]{:S(2)}) async-start(), calls=%async_computation.9 | async-start | bytes 2228224 | tf_op jit(solution)/shard_map/reduce_scatter | solution.py:67
  42.3 1.9 copy-start.3
  42.3 140.4 %reduce-scatter.8.cloned.1.call-start = ((), (), s32[]{:S(2)}) async-start(), calls=%async_computation.10 | async-start | bytes 2228224 | tf_op jit(solution)/shard_map/reduce_scatter | solution.py:66
  44.1 16.4 %copy-start.2 = (bf16[1,2048,224]{1,2,0:T(8,128)(2,1)S(1)}, bf16[1,2048,224]{1,2,0:T(8,128)(2,1)}, u32[]{:S(2)}) copy-start(bf16[1,2048,224]{1,2,0:T(8,128)(2,1)} %param.13) | copy-start | bytes 2752516
  44.1 216.2 %reduce-scatter.4.cloned.1.call-start = ((), (), s32[]{:S(2)}) async-start(), calls=%async_computation.8 | async-start | bytes 2228224 | tf_op jit(solution)/shard_map/reduce_scatter | solution.py:68
  60.5 1.9 copy-start.4
  62.3 274.1 %all-gather.3.cloned.1.call-start = ((), (), s32[]{:S(2)}) async-start(), calls=%async_computation.11 | async-start | bytes 1114112 | tf_op jit(solution)/shard_map/all_gather | solution.py:73
  262.2 147.7 %all-gather.5.cloned.1.call-start = ((), (), s32[]{:S(2)}) async-start(), calls=%async_computation.12 | async-start | bytes 1114112 | tf_op jit(solution)/shard_map/all_gather | solution.py:79
  285.7 126.7 %all-to-all-start.4 = ((bf16[64,1,4]{2,1,0:T(2,128)(2,1)}), bf16[64,1,4]{2,1,0:T(2,128)(2,1)S(1)}, u32[]{:S(2)}, u32[]{:S(2)}) async-start(bf16[64,1,4]{2,1,0:T(2,128)(2,1)} %all_to_all.29), calls=%async_computation.7 | async-start | bytes 65536 | tf_op jit(solution)/shard_map/all_to_all | solution.py:92
  412.4 31.4 %all-to-all-start.3 = ((bf16[64,4,224]{2,1,0:T(4,128)(2,1)}), bf16[64,4,224]{2,1,0:T(4,128)(2,1)S(1)}, u32[]{:S(2)}, u32[]{:S(2)}) async-start(bf16[64,4,224]{2,1,0:T(4,128)(2,1)} %reshape.86), calls=%async_computation.6 | async-start | bytes 262144 | tf_op jit(solution)/shard_map/all_to_all | solution.py:85
Sparse Core Ops, SparseCore 0:
  42.4 63.0 reduce-scatter.5
  108.9 73.7 reduce-scatter.7
  186.1 74.2 reduce-scatter.3
  262.8 73.6 all-gather.2
  338.9 70.9 all-gather.4
where the time goes:
time: 453 us; the launch traced here: 452 us
  waiting for transfers between devices  286 us (63%)
  blocking collectives  79 us (17%)
  starting transfers between devices  48.2 us (11%)
  between operations  14 us (3%)
  local copies, waits for them, and re-layouts  11.8 us (3%)
  matrix products  8.7 us (2%)
    reduce_scatter x1, waiting for transfers between devices, on_device(): lax.psum_scatter(back_part, 'local', scatter_dimension=1, tiled=True)  77.7 us
    reduce_scatter x1, waiting for transfers between devices, on_device(): lax.psum_scatter(gate_part, 'local', scatter_dimension=1, tiled=True)  77.2 us
    all_gather x1, waiting for transfers between devices, on_device(): lax.all_gather(grad_up, 'local', axis=1, tiled=True)  71.7 us
    all_to_all x1, blocking collectives, on_device(): lax.all_to_all(send_rows, 'node', split_axis=0, concat_axis=0, tiled=True)  27.9 us
    reduce_scatter x1, waiting for transfers between devices, on_device(): lax.psum_scatter(up_part, 'local', scatter_dimension=1, tiled=True)  27.2 us
    all_to_all x1, starting transfers between devices, on_device(): lax.all_to_all(prob_grad.reshape(node_count, capacity), 'node', split_axi...  26.9 us
    all_gather x1, waiting for transfers between devices, on_device(): lax.all_gather(grad_gate, 'local', axis=1, tiled=True)  23.8 us
    psum x1, blocking collectives, on_device(): prob_grad = lax.psum(prob_part, 'local').astype(jnp.bfloat16)  22.1 us
  transfers between devices with their start and end apart: 7, of which 6 were waited for; matrix products, arithmetic and copies ran while one was open for 3% of the time, Pallas kernels for 0%

commit v1 on v0

v1 whole, which is shorter than its diff:
```python
import functools
import jax
import jax.numpy as jnp
from jax import lax
from jax.experimental import pallas as pl
from jax.experimental.pallas import tpu as pltpu
from jax.sharding import PartitionSpec as P

CAP = 4
MESH = pl.DeviceIdType.MESH
LANES = 128
PROB_ROWS = 16


def layout(columns):
    wide = -(-(columns + 1) // LANES) * LANES
    return columns, wide


def expert_kernel(
    n, x_ref, wg_ref, wu_ref, wd_ref, out_ref, start, land, ag, acc, rs_send, rs_recv, ag_send, ag_recv
):
    me = lax.axis_index("local")
    half_ring = n // 2
    slots = x_ref.shape[0]
    rows = slots // 2
    columns, wide = layout(wg_ref.shape[0])
    chunk = wg_ref.shape[1] // n
    to = (lax.rem(me + 1, n), lax.rem(me + n - 1, n))

    def wrap(c):
        return lax.rem(c + 2 * n, n)

    barrier = pltpu.get_barrier_semaphore()
    for neighbour in to:
        pl.semaphore_signal(barrier, inc=1, device_id={"local": neighbour}, device_id_type=MESH)
    pl.semaphore_wait(barrier, 2)

    def span(c):
        return pl.ds(pl.multiple_of(c * chunk, chunk), chunk)

    def term(m, h, c):
        own = pl.ds(h * rows, rows)
        if m == 2:
            return lax.dot_general(
                x_ref[own, wide : wide + columns],
                wd_ref[span(c), :],
                (((1,), (1,)), ((), ())),
                preferred_element_type=jnp.float32,
            )
        weight = wg_ref if m == 0 else wu_ref
        return jnp.dot(x_ref[own, 0:columns], weight[:, span(c)], preferred_element_type=jnp.float32)

    def rs_copy(d, s, h, m, source):
        return pltpu.make_async_remote_copy(
            src_ref=source,
            dst_ref=land.at[d, s, h, m],
            send_sem=rs_send.at[d, s, h, m],
            recv_sem=rs_recv.at[d, s, h, m],
            device_id={"local": to[d]},
            device_id_type=MESH,
        )

    def rs_step(s, fresh, carried):
        chunk_of = (wrap(me + half_ring - s), wrap(me - half_ring + s))
        for h in range(2):
            for m in range(3):
                for d in range(2):
                    if (d, h) in fresh:
                        start[d, h, m] = term(m, h, chunk_of[d]).astype(jnp.bfloat16)
                        rs_copy(d, s, h, m, start.at[d, h, m]).start()
                    elif (d, h) in carried:
                        own = term(m, h, chunk_of[d])
                        held = land.at[d, s - 1, h, m]
                        rs_copy(d, s - 1, h, m, held).wait_recv()
                        held[...] = (own + held[...].astype(jnp.float32)).astype(jnp.bfloat16)
                        rs_copy(d, s, h, m, held).start()

    longer = ((0, 0), (1, 1))
    shorter = ((0, 1), (1, 0))
    rs_step(0, longer, ())
    rs_step(1, shorter, longer)

    def rs_body(s, carry):
        rs_step(s, (), longer + shorter)
        return carry

    lax.fori_loop(2, half_ring, rs_body, 0)

    def ag_copy(d, t, h, part):
        c = wrap(me - t) if d == 0 else wrap(me + t)
        block = ag.at[c, h, pl.ds(0, rows)] if part == 0 else ag.at[c, h, pl.ds(rows, rows + PROB_ROWS)]
        return pltpu.make_async_remote_copy(
            src_ref=block,
            dst_ref=block,
            send_sem=ag_send.at[d, t, h, part],
            recv_sem=ag_recv.at[d, t, h, part],
            device_id={"local": to[d]},
            device_id_type=MESH,
        )

    def ag_wait(d, t, h, part):
        c = wrap(me - 1 - t) if d == 0 else wrap(me + 1 + t)
        block = ag.at[c, h, pl.ds(0, rows)] if part == 0 else ag.at[c, h, pl.ds(rows, rows + PROB_ROWS)]
        pltpu.make_async_remote_copy(
            src_ref=block,
            dst_ref=block,
            send_sem=ag_send.at[d, t, h, part],
            recv_sem=ag_recv.at[d, t, h, part],
            device_id={"local": to[d]},
            device_id_type=MESH,
        ).wait_recv()
        return c

    def product(c, h):
        dims = (((1,), (1,)), ((), ()))
        return lax.dot_general(
            ag[c, h, 0:rows], wg_ref[:, span(c)], dims, preferred_element_type=jnp.float32
        ) + lax.dot_general(
            ag[c, h, rows : 2 * rows], wu_ref[:, span(c)], dims, preferred_element_type=jnp.float32
        )

    last = half_ring - 1
    for h in range(2):
        sums = []
        for m in range(3):
            total = term(m, h, me)
            for d in range(2):
                rs_copy(d, last, h, m, land.at[d, last, h, m]).wait_recv()
                total = total + land[d, last, h, m].astype(jnp.float32)
            sums.append(total)
        gate, up, back = sums
        prob = x_ref[pl.ds(h * rows, rows), columns : columns + 1].astype(jnp.float32)
        squash = jax.nn.sigmoid(gate)
        gated = gate * squash
        hidden = back * prob
        ag[me, h, 0:rows] = (hidden * up * squash * (1.0 + gate * (1.0 - squash))).astype(jnp.bfloat16)
        for d in range(2):
            ag_copy(d, 0, h, 0).start()
        ag[me, h, rows : 2 * rows] = (hidden * gated).astype(jnp.bfloat16)
        both = gated * up * back
        high = both.astype(jnp.bfloat16)
        low = (both - high.astype(jnp.float32)).astype(jnp.bfloat16)
        ones = jnp.ones((8, chunk), jnp.bfloat16)
        dims = (((1,), (1,)), ((), ()))
        part = lax.dot_general(ones, high, dims, preferred_element_type=jnp.float32) + lax.dot_general(
            ones, low, dims, preferred_element_type=jnp.float32
        )
        part_high = part.astype(jnp.bfloat16).astype(jnp.float32)
        both_parts = jnp.concatenate([part_high, part - part_high], axis=0).astype(jnp.bfloat16)
        ag[me, h, 2 * rows : 2 * rows + PROB_ROWS] = both_parts
        for d in range(2):
            ag_copy(d, 0, h, 1).start()
    for h in range(2):
        acc[h] = product(me, h)

    def ag_step(t, forwarded, received):
        for h in range(2):
            came = []
            for part in range(2):
                for d in range(2):
                    if (d, h) in received:
                        c = ag_wait(d, t - 1, h, part)
                        if part == 1:
                            came.append(c)
                    if (d, h) in forwarded:
                        ag_copy(d, t, h, part).start()
            total = acc[h]
            for c in came:
                total = total + product(c, h)
            acc[h] = total

    def ag_body(t, carry):
        ag_step(t, longer + shorter, longer + shorter)
        return carry

    lax.fori_loop(1, half_ring - 1, ag_body, 0)
    ag_step(half_ring - 1, longer, longer + shorter)
    ag_step(half_ring, (), longer)

    for h in range(2):
        parts = jnp.sum(ag[:, h, 2 * rows : 2 * rows + PROB_ROWS].astype(jnp.float32), axis=0)
        whole = parts[0:8] + parts[8:16]
        spread = jnp.transpose(jnp.broadcast_to(whole[0:1], (LANES, rows)))
        out_ref[pl.ds(h * rows, rows), 0:columns] = acc[h].astype(jnp.bfloat16)
        out_ref[pl.ds(h * rows, rows), columns:wide] = spread[:, columns % LANES :].astype(jnp.bfloat16)

    def drain_rs(s, pairs):
        for d, h in pairs:
            for m in range(3):
                rs_copy(d, s, h, m, land.at[d, s, h, m]).wait_send()

    def drain_ag(t, pairs):
        for d, h in pairs:
            for part in range(2):
                ag_copy(d, t, h, part).wait_send()

    drain_rs(0, longer)

    def drain_body(s, carry):
        drain_rs(s, longer + shorter)
        drain_ag(s - 1, longer + shorter)
        return carry

    lax.fori_loop(1, half_ring, drain_body, 0)
    drain_ag(half_ring - 1, longer)


def expert(x, w_gate, w_up, w_down):
    n = lax.axis_size("local")
    slots = x.shape[0]
    columns, wide = layout(w_gate.shape[0])
    rows, chunk, half_ring = slots // 2, w_gate.shape[1] // n, n // 2
    vmem = pl.BlockSpec(memory_space=pltpu.VMEM)
    return pl.pallas_call(
        functools.partial(expert_kernel, n),
        out_shape=jax.ShapeDtypeStruct((slots, wide), jnp.bfloat16),
        in_specs=[vmem] * 4,
        out_specs=vmem,
        scratch_shapes=[
            pltpu.VMEM((2, 2, 3, rows, chunk), jnp.bfloat16),
            pltpu.VMEM((2, half_ring, 2, 3, rows, chunk), jnp.bfloat16),
            pltpu.VMEM((n, 2, 2 * rows + PROB_ROWS, chunk), jnp.bfloat16),
            pltpu.VMEM((2, rows, columns), jnp.float32),
            pltpu.SemaphoreType.DMA((2, half_ring, 2, 3)),
            pltpu.SemaphoreType.DMA((2, half_ring, 2, 3)),
            pltpu.SemaphoreType.DMA((2, half_ring, 2, 2)),
            pltpu.SemaphoreType.DMA((2, half_ring, 2, 2)),
        ],
        compiler_params=pltpu.CompilerParams(
            collective_id=0, has_side_effects=True, vmem_limit_bytes=40 * 1024 * 1024
        ),
    )(x, w_gate, w_up, w_down)


def on_device(tokens, grad_out, route_prob, route_expert, w_gate, w_up, w_down):
    node_count = lax.axis_size("node")
    node_tokens, top_count = route_expert.shape
    columns, wide = layout(tokens.shape[1])
    slots = node_count * CAP
    lane = jnp.arange(slots, dtype=jnp.int32)[None, :]
    named = [route_expert[:, k : k + 1] == lane // CAP for k in range(top_count)]
    hits = functools.reduce(jnp.logical_or, named).astype(jnp.bfloat16)
    order = jnp.arange(node_tokens, dtype=jnp.int32)
    earlier = (order[None, :] < order[:, None]).astype(jnp.bfloat16)
    rank = jnp.dot(earlier, hits, preferred_element_type=jnp.float32)
    fits = rank == (lane % CAP).astype(jnp.float32)
    place = jnp.concatenate([(one & fits) for one in named], axis=0).astype(jnp.bfloat16)
    blank = jnp.zeros((node_tokens, wide - columns - 1), jnp.bfloat16)
    blank_wide = jnp.zeros((node_tokens, wide - columns), jnp.bfloat16)
    source = jnp.concatenate(
        [
            jnp.concatenate([tokens, route_prob[:, k : k + 1], blank, grad_out, blank_wide], axis=1)
            for k in range(top_count)
        ],
        axis=0,
    )
    send = lax.dot_general(
        place, source, (((0,), (0,)), ((), ())), preferred_element_type=jnp.float32
    ).astype(jnp.bfloat16)
    arrived = lax.all_to_all(
        send.reshape(node_count, CAP, 2 * wide), "node", split_axis=0, concat_axis=0, tiled=True
    ).reshape(slots, 2 * wide)
    result = expert(arrived, w_gate[0], w_up[0], w_down[0])
    returned = lax.all_to_all(
        result.reshape(node_count, CAP, wide), "node", split_axis=0, concat_axis=0, tiled=True
    ).reshape(slots, wide)
    picked = jnp.dot(place, returned, preferred_element_type=jnp.float32).reshape(
        top_count, node_tokens, wide
    )
    grad_tokens = jnp.sum(picked[:, :, 0:columns], axis=0).astype(jnp.bfloat16)
    grad_prob = picked[:, :, columns].T.astype(jnp.bfloat16)
    return grad_tokens, grad_prob


def solution(mesh):
    return jax.shard_map(
        on_device,
        mesh=mesh,
        in_specs=(
            P("node", "local"),
            P("node", "local"),
            P("node", None),
            P("node", None),
            P("node", "local", None),
            P("node", "local", None),
            P("node", None, "local"),
        ),
        out_specs=(P("node", "local"), P("node", None)),
        check_vma=False,
    )
```

time: 453 us -> 131 us (0.29)
  waiting for transfers between devices: 286 us -> 20.8 us
  blocking collectives: 79 us -> 0 us
  Pallas kernels: 0 us -> 70.3 us
  starting transfers between devices: 48.2 us -> 30.5 us
  between operations: 14 us -> 0.76 us
  matrix products: 8.7 us -> 0.65 us
  local copies, waits for them, and re-layouts: 11.8 us -> 6.54 us
    reduce_scatter x3 -> x0, waiting for transfers between devices: 182 us -> none  [the longest x1 77.7 us: on_device(): lax.psum_scatter(back_part, 'local', scatter_dimension=1, tiled=True)]
    all_gather x2 -> x0, waiting for transfers between devices: 95.5 us -> none  [the longest x1 71.7 us: on_device(): lax.all_gather(grad_up, 'local', axis=1, tiled=True)]
    pallas_call x0 -> x1, Pallas kernels: none -> 70.3 us  [expert(): pl.pallas_call(functools.partial(expert_kernel, n), out_shape=jax.ShapeDt...]
    all_to_all x3 -> x0, blocking collectives: 56.9 us -> none  [the longest x1 27.9 us: on_device(): lax.all_to_all(send_rows, 'node', split_axis=0, concat_axis=0, tiled=True)]
    psum x1 -> x0, blocking collectives: 22.1 us -> none  [on_device(): prob_grad = lax.psum(prob_part, 'local').astype(jnp.bfloat16)]
    all_to_all x2, starting transfers between devices: 48 us -> 30.5 us  [the longest x1 18.2 us: on_device(): lax.all_to_all(send.reshape(node_count, CAP, 2 * wide), 'node', split_axi...]
    all_to_all x2, waiting for transfers between devices: 8.12 us -> 20.8 us  [the longest x1 10.4 us: on_device(): lax.all_to_all(send.reshape(node_count, CAP, 2 * wide), 'node', split_axi...]
    dot_general x5 -> x3, matrix products: 8.7 us -> 0.65 us  [the longest x1 0.27 us: on_device(): lax.dot_general(place, source, (((0,), (0,)), ((), ())), preferred_elemen...]
  transfers between devices with their start and end apart: 7 -> 2, of which waited for: 6 -> 2; matrix products, arithmetic and copies ran while one was open for 3% -> 1% of each run, Pallas kernels for 0% -> 0%
where the time goes in v1:
time: 131 us; the launch traced here: 130 us
  Pallas kernels  70.3 us (54%)
  starting transfers between devices  30.5 us (23%)
  waiting for transfers between devices  20.8 us (16%)
  local copies, waits for them, and re-layouts  6.54 us (5%)
    pallas_call x1, Pallas kernels, expert(): pl.pallas_call(functools.partial(expert_kernel, n), out_shape=jax.ShapeDt...  70.3 us
    all_to_all x1, starting transfers between devices, on_device(): lax.all_to_all(send.reshape(node_count, CAP, 2 * wide), 'node', split_axi...  18.2 us
    all_to_all x1, starting transfers between devices, on_device(): lax.all_to_all(result.reshape(node_count, CAP, wide), 'node', split_axis=...  12.3 us
    all_to_all x1, waiting for transfers between devices, on_device(): lax.all_to_all(send.reshape(node_count, CAP, 2 * wide), 'node', split_axi...  10.4 us
    all_to_all x1, waiting for transfers between devices, on_device(): lax.all_to_all(result.reshape(node_count, CAP, wide), 'node', split_axis=...  10.3 us
    unnamed x13, local copies, waits for them, and re-layouts  3.46 us
  transfers between devices with their start and end apart: 2, of which 2 were waited for; matrix products, arithmetic and copies ran while one was open for 1% of the time, Pallas kernels for 0%

profile of v1, /device:TPU:1, one launch (start us, length us, event | category | flops | bytes accessed | tf_op | source)
XLA Modules:
  0.0 130.1 jit_solution(14099952095675617052)
XLA Ops:
  0.6 0.0 copy-start.4
  0.7 0.7 copy-done.4
  1.3 0.0 copy-start.5
  1.3 0.7 copy-done.5
  2.0 0.1 copy.14
  2.1 0.1 copy.15
  2.2 0.1 copy.17
  2.3 0.1 copy.16
  2.4 0.5 copy-done.2
  2.9 0.0 copy-done.3
  2.9 0.1 concatenate.21
  3.0 0.1 concatenate.22
  3.1 0.1 concatenate.20
  3.2 0.1 concatenate.19
  3.3 0.2 compare_and_fusion.3
  3.5 0.3 convolution_convert_fusion
  3.8 0.8 reshape.73
  4.6 18.2 %all-to-all-start = ((bf16[64,4,512]{2,1,0:T(4,128)(2,1)}), bf16[64,4,512]{2,1,0:T(4,128)(2,1)S(1)}, u32[]{:S(2)}, u32[]{:S(2)}) async-start(bf16[64,4,512]{2,1,0:T(4,128)(2,1)} %reshape.73), calls=%async_computation | async-start | bytes 524288 | tf_op jit(solution)/shard_map/all_to_all | solution.py:261
  22.8 0.0 copy-start
  22.8 0.0 copy-start.1
  22.8 1.6 %copy.18 = bf16[1,2048,224]{2,1,0:T(8,128)(2,1)S(1)} copy(bf16[1,2048,224]{1,2,0:T(8,128)(2,1)} %param.13) | data formatting | bytes 1835008 | tf_op args[6]
  24.4 10.4 %all-to-all-done = bf16[64,4,512]{2,1,0:T(4,128)(2,1)S(1)} async-done(((bf16[64,4,512]{2,1,0:T(4,128)(2,1)}), bf16[64,4,512]{2,1,0:T(4,128)(2,1)S(1)}, u32[]{:S(2)}, u32[]{:S(2)}) %all-to-all-start) | async-done | bytes 262176 | tf_op jit(solution)/shard_map/all_to_all | solution.py:261
  34.8 0.1 reshape.74.x_ref
  34.9 0.0 copy-done
  34.9 0.0 copy-done.1
  34.9 70.3 %shard_map.86 = bf16[256,256]{1,0:T(8,128)(2,1)S(1)} custom-call(bf16[256,512]{1,0:T(8,128)(2,1)S(1)} %reshape.74.x_ref, bf16[224,2048]{1,0:T(8,128)(2,1)S(1)} %bitcast.16, bf16[224,2048]{1,0:T(8,128)(2,1)S(1)} %bitcast.17, bf16[2048,224]{1,0:T(8,128)(2,1)S(1)} %bitcast.15), custom_call_target="tpu_custom_call" | custom-call | tf_op jit(solution)/shard_map/pallas_call | solution.py:215
  105.2 0.7 reshape.75
  105.9 12.3 %all-to-all-start.1 = ((bf16[64,4,256]{2,1,0:T(4,128)(2,1)}), bf16[64,4,256]{2,1,0:T(4,128)(2,1)S(1)}, u32[]{:S(2)}, u32[]{:S(2)}) async-start(bf16[64,4,256]{2,1,0:T(4,128)(2,1)} %reshape.75), calls=%async_computation.1 | async-start | bytes 262144 | tf_op jit(solution)/shard_map/all_to_all | solution.py:265
  118.2 10.3 %all-to-all-done.1 = bf16[64,4,256]{2,1,0:T(4,128)(2,1)S(1)} async-done(((bf16[64,4,256]{2,1,0:T(4,128)(2,1)}), bf16[64,4,256]{2,1,0:T(4,128)(2,1)S(1)}, u32[]{:S(2)}, u32[]{:S(2)}) %all-to-all-start.1) | async-done | bytes 131104 | tf_op jit(solution)/shard_map/all_to_all | solution.py:265
  128.6 0.2 fusion.18
  128.8 0.7 fusion.7
  129.5 0.6 slice_reduce_fusion
  (9 shorter events, 0.1 us)
Async XLA Ops:
  0.6 0.7 copy-start.4
  1.3 0.7 copy-start.5
  2.2 0.7 copy-start.2
  2.2 0.7 copy-start.3
  4.6 30.2 %all-to-all-start = ((bf16[64,4,512]{2,1,0:T(4,128)(2,1)}), bf16[64,4,512]{2,1,0:T(4,128)(2,1)S(1)}, u32[]{:S(2)}, u32[]{:S(2)}) async-start(bf16[64,4,512]{2,1,0:T(4,128)(2,1)} %reshape.73), calls=%async_computation | async-start | bytes 524288 | tf_op jit(solution)/shard_map/all_to_all | solution.py:261
  22.8 12.1 %copy-start = (bf16[1,224,2048]{2,1,0:T(8,128)(2,1)S(1)}, bf16[1,224,2048]{2,1,0:T(8,128)(2,1)}, u32[]{:S(2)}) copy-start(bf16[1,224,2048]{2,1,0:T(8,128)(2,1)} %param.11) | copy-start | bytes 2752516
  22.8 12.1 %copy-start.1 = (bf16[1,224,2048]{2,1,0:T(8,128)(2,1)S(1)}, bf16[1,224,2048]{2,1,0:T(8,128)(2,1)}, u32[]{:S(2)}) copy-start(bf16[1,224,2048]{2,1,0:T(8,128)(2,1)} %param.12) | copy-start | bytes 2752516
  105.9 22.7 %all-to-all-start.1 = ((bf16[64,4,256]{2,1,0:T(4,128)(2,1)}), bf16[64,4,256]{2,1,0:T(4,128)(2,1)S(1)}, u32[]{:S(2)}, u32[]{:S(2)}) async-start(bf16[64,4,256]{2,1,0:T(4,128)(2,1)} %reshape.75), calls=%async_computation.1 | async-start | bytes 262144 | tf_op jit(solution)/shard_map/all_to_all | solution.py:265

commit v2 on v0

v2 whole, which is shorter than its diff:
```python
import functools
import jax
import jax.numpy as jnp
from jax import lax
from jax.experimental import pallas as pl
from jax.experimental.pallas import tpu as pltpu
from jax.sharding import PartitionSpec as P

CAP = 4
MESH = pl.DeviceIdType.MESH
LANES = 128
BF16, F32 = jnp.bfloat16, jnp.float32
CROSS = (((1,), (1,)), ((), ()))


def iota(shape, dim):
    return lax.broadcasted_iota(jnp.int32, shape, dim)


def ones_where(mask):
    return jnp.where(mask, 1.0, 0.0).astype(BF16)


def mult(a, b):
    return jnp.dot(a, b, preferred_element_type=F32)


def moe_kernel(
    nodes, n, tok_ref, grad_ref, prob_ref, route_ref, wg_hbm, wu_hbm, wd_hbm, dx_ref, dp_ref,
    wg, wu, wd, outbox, inbox, xs, terms, start, land, ag, pp, acc, outbox2, inbox2,
    w_sem, out_send, out_recv, rs_send, rs_recv, ag_send, ag_recv, back_send, back_recv,
):
    node, me = lax.axis_index("node"), lax.axis_index("local")
    half_ring = n // 2
    slots = nodes * CAP
    rows = slots // 2
    piece = rows // 2
    columns = tok_ref.shape[1]
    rest = columns - LANES
    top, tokens = route_ref.shape
    pairs = top * tokens
    chunk = wg.shape[1] // n
    to = (lax.rem(me + 1, n), lax.rem(me + n - 1, n))

    loads = [
        pltpu.make_async_copy(source, kept, w_sem.at[i])
        for i, (source, kept) in enumerate(((wg_hbm, wg), (wu_hbm, wu), (wd_hbm, wd)))
    ]
    for load in loads:
        load.start()

    barrier = pltpu.get_barrier_semaphore()

    def greet(i, carry):
        pl.semaphore_signal(
            barrier, inc=1, device_id={"node": lax.rem(node + i, nodes)}, device_id_type=MESH
        )
        return carry

    lax.fori_loop(1, nodes, greet, 0)
    for neighbour in to:
        pl.semaphore_signal(barrier, inc=1, device_id={"local": neighbour}, device_id_type=MESH)

    def flat(ref):
        kept = ref[...].astype(F32)
        return jnp.concatenate([kept[k : k + 1] for k in range(top)], axis=1)

    diagonal = iota((pairs, pairs), 0) == iota((pairs, pairs), 1)

    def upright(row):
        return jnp.sum(jnp.where(diagonal, row, 0.0), axis=1, keepdims=True)

    expert_row = flat(route_ref)
    expert_col = upright(expert_row)
    same = expert_row == expert_col
    token_down, token_along = iota((pairs, pairs), 0) % tokens, iota((pairs, pairs), 1) % tokens
    rank_row = jnp.sum(jnp.where(same & (token_down < token_along), 1.0, 0.0), axis=0, keepdims=True)
    rank_col = jnp.sum(jnp.where(same & (token_along < token_down), 1.0, 0.0), axis=1, keepdims=True)
    prob_col = upright(flat(prob_ref))

    blank = jnp.zeros((tokens, LANES - rest), F32)
    lane = iota((pairs, LANES), 1)

    def stacked(block):
        return jnp.concatenate([block] * top, axis=0)

    held_tokens, held_grads = tok_ref[...].astype(F32), grad_ref[...].astype(F32)
    source = jnp.concatenate(
        [
            stacked(held_tokens[:, 0:LANES]),
            jnp.where(
                lane == rest,
                prob_col,
                stacked(jnp.concatenate([held_tokens[:, LANES:columns], blank], axis=1)),
            ),
            stacked(held_grads[:, 0:LANES]),
            stacked(jnp.concatenate([held_grads[:, LANES:columns], blank], axis=1)),
        ],
        axis=0,
    ).astype(BF16)
    target = (expert_row * (4 * CAP) + rank_row).astype(jnp.int32)
    targets = jnp.concatenate([target + CAP * j for j in range(4)], axis=1)
    place = ones_where(iota((4 * slots, 4 * pairs), 0) == targets)
    outbox[...] = mult(place, source).astype(BF16).reshape(outbox.shape)
    inbox[node] = outbox[node]

    pl.semaphore_wait(barrier, nodes + 1)

    def send_copy(peer):
        return pltpu.make_async_remote_copy(
            src_ref=outbox.at[peer],
            dst_ref=inbox.at[node],
            send_sem=out_send,
            recv_sem=out_recv,
            device_id={"node": peer},
            device_id_type=MESH,
        )

    def send_body(i, carry):
        send_copy(lax.rem(node + i, nodes)).start()
        return carry

    lax.fori_loop(1, nodes, send_body, 0)

    group = 64 // CAP
    down, along = iota((256, 256), 0), iota((256, 256), 1)
    sender, rest_of = along // (4 * CAP), along % (4 * CAP)
    order_in = ones_where(down == 64 * (rest_of // CAP) + CAP * sender + rest_of % CAP)
    sender2, rest_of2 = down // (2 * CAP), down % (2 * CAP)
    order_out = ones_where(along == rows * (rest_of2 // CAP) + CAP * sender2 + rest_of2 % CAP)
    target2 = (expert_col * (2 * CAP) + rank_col).astype(jnp.int32)
    targets2 = jnp.concatenate([target2, target2 + CAP], axis=0)
    pick = ones_where(iota((2 * pairs, 2 * slots), 1) == targets2)

    for load in loads:
        load.wait()

    def all_of(send, recv, source, into):
        return pltpu.make_async_remote_copy(
            src_ref=source.at[pl.ds(0, nodes - 1)],
            dst_ref=into.at[pl.ds(0, nodes - 1)],
            send_sem=send,
            recv_sem=recv,
            device_id={"node": lax.rem(node + 1, nodes)},
            device_id_type=MESH,
        )

    all_of(out_send, out_recv, outbox, inbox).wait_recv()
    arrived = inbox[...].reshape(4 * slots, LANES)
    blocks = slots // 64
    mixed = mult(
        order_in, jnp.concatenate([arrived[256 * g : 256 * g + 256] for g in range(blocks)], axis=1)
    ).astype(BF16)
    for g in range(blocks):
        for j in range(4):
            xs[64 * g : 64 * g + 64, LANES * j : LANES * (j + 1)] = mixed[
                64 * j : 64 * j + 64, LANES * g : LANES * (g + 1)
            ]

    def wrap(c):
        return lax.rem(c + 2 * n, n)

    def span(c):
        return pl.ds(pl.multiple_of(c * chunk, chunk), chunk)

    def term(m, c):
        if m == 2:
            return mult(xs[:, 2 * LANES : 2 * LANES + columns], wd[:, span(c)])
        return mult(xs[:, 0:columns], (wg, wu)[m][:, span(c)])

    def own_rows(h):
        return pl.ds(h * rows, rows)

    def rs_copy(d, s, h, m, source):
        return pltpu.make_async_remote_copy(
            src_ref=source,
            dst_ref=land.at[d, s, h, m],
            send_sem=rs_send.at[d, s, h, m],
            recv_sem=rs_recv.at[d, s, h, m],
            device_id={"local": to[d]},
            device_id_type=MESH,
        )

    def chunks_at(s):
        return (wrap(me + half_ring - s), wrap(me - half_ring + s))

    def terms_for(s):
        for d, c in enumerate(chunks_at(s)):
            for m in range(3):
                terms[d, m] = term(m, c)

    longer = ((0, 0), (1, 1))
    shorter = ((0, 1), (1, 0))

    def rs_step(s, fresh):
        for h in range(2):
            for m in range(3):
                for d in range(2):
                    own = terms[d, m, own_rows(h)]
                    if (d, h) in fresh:
                        start[d, h, m] = own.astype(BF16)
                        rs_copy(d, s, h, m, start.at[d, h, m]).start()
                    else:
                        held = land.at[d, s - 1, h, m]
                        rs_copy(d, s - 1, h, m, held).wait_recv()
                        held[...] = (own + held[...].astype(F32)).astype(BF16)
                        rs_copy(d, s, h, m, held).start()

    for m in range(3):
        both = term(m, wrap(me + half_ring))
        for d, h in longer:
            start[d, h, m] = both[h * rows : (h + 1) * rows].astype(BF16)
            rs_copy(d, 0, h, m, start.at[d, h, m]).start()
    terms_for(1)
    rs_step(1, shorter)

    def rs_body(s, carry):
        terms_for(s)
        rs_step(s, ())
        return carry

    lax.fori_loop(2, half_ring, rs_body, 0)
    for m in range(3):
        terms[0, m] = term(m, me)

    order = (0, 1, 4, 2, 3)

    def is_longer(d, q):
        return d == (0 if q < 2 else 1)

    def ag_copy(d, t, q, c):
        block = pp.at[c] if q == 4 else ag.at[c, pl.ds(q * piece, piece)]
        return pltpu.make_async_remote_copy(
            src_ref=block,
            dst_ref=block,
            send_sem=ag_send.at[d, t, q],
            recv_sem=ag_recv.at[d, t, q],
            device_id={"local": to[d]},
            device_id_type=MESH,
        )

    def sent_at(d, t):
        return wrap(me - t) if d == 0 else wrap(me + t)

    def ag_wait(d, t, q):
        ag_copy(d, t, q, sent_at(d, t + 1)).wait_recv()

    def product(c, first, count):
        weights = jnp.concatenate([wg[:, span(c)], wu[:, span(c)]], axis=1)
        return lax.dot_general(
            ag[c, pl.ds(first, count)], weights, CROSS, preferred_element_type=F32
        )

    last = half_ring - 1
    for h in range(2):
        sums = []
        for m in range(3):
            total = terms[0, m, own_rows(h)]
            for d in range(2):
                rs_copy(d, last, h, m, land.at[d, last, h, m]).wait_recv()
                total = total + land[d, last, h, m].astype(F32)
            sums.append(total)
        gate, up, back = sums
        prob = xs[own_rows(h), columns : columns + 1].astype(F32)
        squash = jax.nn.sigmoid(gate)
        gated = gate * squash
        hidden = back * prob
        ag[me, own_rows(h), 0:chunk] = (
            hidden * up * squash * (1.0 + gate * (1.0 - squash))
        ).astype(BF16)
        ag[me, own_rows(h), chunk : 2 * chunk] = (hidden * gated).astype(BF16)
        if h == 0:
            for q in (0, 1):
                for d in range(2):
                    ag_copy(d, 0, q, me).start()
        both = gated * up * back
        high = both.astype(BF16)
        low = (both - high.astype(F32)).astype(BF16)
        ones = jnp.ones((8, chunk), BF16)
        part = lax.dot_general(ones, high, CROSS, preferred_element_type=F32) + lax.dot_general(
            ones, low, CROSS, preferred_element_type=F32
        )
        pp[me, 4 * h : 4 * h + 4] = part[0:4]
    for q in (4, 2, 3):
        for d in range(2):
            ag_copy(d, 0, q, me).start()
    acc[...] = product(me, 0, slots)

    def ag_step(t, all_forwarded):
        for q in order:
            for d in range(2):
                ag_wait(d, t - 1, q)
                if all_forwarded or is_longer(d, q):
                    ag_copy(d, t, q, sent_at(d, t)).start()
        acc[...] += product(sent_at(0, t), 0, slots) + product(sent_at(1, t), 0, slots)

    def ag_body(t, carry):
        ag_step(t, True)
        return carry

    lax.fori_loop(1, half_ring - 1, ag_body, 0)
    ag_step(half_ring - 1, False)

    def back_copy(peer):
        return pltpu.make_async_remote_copy(
            src_ref=outbox2.at[peer],
            dst_ref=inbox2.at[node],
            send_sem=back_send,
            recv_sem=back_recv,
            device_id={"node": peer},
            device_id_type=MESH,
        )

    farthest = wrap(me + half_ring)
    for h in range(2):
        for q in (2 * h, 2 * h + 1):
            ag_wait(h, last, q)
        total = acc[own_rows(h)] + product(farthest, h * rows, rows)
        if h == 0:
            ag_wait(1, last, 4)
            weight_sums = jnp.sum(pp[...], axis=0)
        spread = jnp.transpose(jnp.broadcast_to(weight_sums[4 * h : 4 * h + 1], (LANES, rows)))
        stack = jnp.concatenate(
            [
                total[:, 0:LANES],
                jnp.concatenate([total[:, LANES:columns], spread[:, rest:LANES]], axis=1),
            ],
            axis=0,
        ).astype(BF16)
        half = nodes // 2
        outbox2[h * half : (h + 1) * half] = (
            mult(order_out, stack).reshape((half,) + outbox2.shape[1:]).astype(BF16)
        )

        def back_body(i, carry, h=h, half=half):
            peer = h * half + lax.rem(node + i, half)

            @pl.when(peer != node)
            def _():
                back_copy(peer).start()

            return carry

        lax.fori_loop(0, half, back_body, 0)
    inbox2[node] = outbox2[node]

    all_of(back_send, back_recv, outbox2, inbox2).wait_recv()
    returned = inbox2[...].astype(F32).reshape(2 * slots, LANES).astype(BF16)
    picked = mult(pick, returned)
    low_sum, high_sum = picked[0:tokens], picked[pairs : pairs + tokens]
    for k in range(1, top):
        low_sum += picked[k * tokens : (k + 1) * tokens]
        high_sum += picked[pairs + k * tokens : pairs + (k + 1) * tokens]
    dx_ref[:, 0:LANES] = low_sum.astype(BF16)
    dx_ref[:, LANES:columns] = high_sum[:, 0:rest].astype(BF16)
    prob_grad = picked[pairs : 2 * pairs, rest : rest + 1]
    along_row = jnp.sum(jnp.where(diagonal, prob_grad, 0.0), axis=0, keepdims=True)
    dp_ref[...] = jnp.concatenate(
        [along_row[:, k * tokens : (k + 1) * tokens] for k in range(top)], axis=0
    ).astype(BF16)

    all_of(out_send, out_recv, outbox, inbox).wait_send()
    all_of(back_send, back_recv, outbox2, inbox2).wait_send()

    def drain(s, rs_streams, ag_all):
        for d, h in rs_streams:
            for m in range(3):
                rs_copy(d, s, h, m, land.at[d, s, h, m]).wait_send()
        for q in order:
            for d in range(2):
                if ag_all or is_longer(d, q):
                    ag_copy(d, s, q, me).wait_send()

    drain(0, longer, True)

    def drain_body(s, carry):
        drain(s, longer + shorter, True)
        return carry

    lax.fori_loop(1, half_ring - 1, drain_body, 0)
    drain(half_ring - 1, longer + shorter, False)


def on_device(tokens, grad_out, route_prob, route_expert, w_gate, w_up, w_down):
    nodes, n = lax.axis_size("node"), lax.axis_size("local")
    slots = nodes * CAP
    width, hidden = w_gate.shape[1:]
    rows, chunk, half_ring = slots // 2, hidden // n, n // 2
    vmem, hbm = pl.BlockSpec(memory_space=pltpu.VMEM), pl.BlockSpec(memory_space=pl.ANY)
    block_tokens, top = route_expert.shape
    dma = pltpu.SemaphoreType.DMA
    grad_tokens, grad_prob = pl.pallas_call(
        functools.partial(moe_kernel, nodes, n),
        out_shape=(
            jax.ShapeDtypeStruct(tokens.shape, BF16),
            jax.ShapeDtypeStruct((top, block_tokens), BF16),
        ),
        in_specs=[vmem] * 4 + [hbm] * 3,
        out_specs=(vmem, vmem),
        scratch_shapes=[
            pltpu.VMEM((width, hidden), BF16),
            pltpu.VMEM((width, hidden), BF16),
            pltpu.VMEM((width, hidden), BF16),
            pltpu.VMEM((nodes, 4 * CAP, LANES), BF16),
            pltpu.VMEM((nodes, 4 * CAP, LANES), BF16),
            pltpu.VMEM((slots, 4 * LANES), BF16),
            pltpu.VMEM((2, 3, slots, chunk), F32),
            pltpu.VMEM((2, 2, 3, rows, chunk), BF16),
            pltpu.VMEM((2, half_ring, 2, 3, rows, chunk), BF16),
            pltpu.VMEM((n, slots, 2 * chunk), BF16),
            pltpu.VMEM((n, 8, LANES), F32),
            pltpu.VMEM((slots, width), F32),
            pltpu.VMEM((nodes, 2 * CAP, LANES), BF16),
            pltpu.VMEM((nodes, 2 * CAP, LANES), BF16),
            dma((3,)),
            dma,
            dma,
            dma((2, half_ring, 2, 3)),
            dma((2, half_ring, 2, 3)),
            dma((2, half_ring, 5)),
            dma((2, half_ring, 5)),
            dma,
            dma,
        ],
        compiler_params=pltpu.CompilerParams(
            collective_id=0, has_side_effects=True, vmem_limit_bytes=56 * 1024 * 1024
        ),
    )(
        tokens,
        grad_out,
        route_prob.T,
        route_expert.T,
        w_gate[0],
        w_up[0],
        jnp.swapaxes(w_down[0], 0, 1),
    )
    return grad_tokens, grad_prob.T


def solution(mesh):
    return jax.shard_map(
        on_device,
        mesh=mesh,
        in_specs=(
            P("node", "local"),
            P("node", "local"),
            P("node", None),
            P("node", None),
            P("node", "local", None),
            P("node", "local", None),
            P("node", None, "local"),
        ),
        out_specs=(P("node", "local"), P("node", None)),
        check_vma=False,
    )
```

time: 453 us -> 113 us (0.25)
  waiting for transfers between devices: 286 us -> 0 us
  Pallas kernels: 0 us -> 110 us
  blocking collectives: 79 us -> 0 us
  starting transfers between devices: 48.2 us -> 0 us
  between operations: 14 us -> 0.65 us
  local copies, waits for them, and re-layouts: 11.8 us -> 1.89 us
  matrix products: 8.7 us -> 0 us
    reduce_scatter x3 -> x0, waiting for transfers between devices: 182 us -> none  [the longest x1 77.7 us: on_device(): lax.psum_scatter(back_part, 'local', scatter_dimension=1, tiled=True)]
    pallas_call x0 -> x1, Pallas kernels: none -> 110 us  [on_device(): pl.pallas_call(functools.partial(moe_kernel, nodes, n), out_shape=(jax.Sh...]
    all_gather x2 -> x0, waiting for transfers between devices: 95.5 us -> none  [the longest x1 71.7 us: on_device(): lax.all_gather(grad_up, 'local', axis=1, tiled=True)]
    all_to_all x3 -> x0, blocking collectives: 56.9 us -> none  [the longest x1 27.9 us: on_device(): lax.all_to_all(send_rows, 'node', split_axis=0, concat_axis=0, tiled=True)]
    all_to_all x2 -> x0, starting transfers between devices: 48 us -> none  [the longest x1 26.9 us: on_device(): lax.all_to_all(prob_grad.reshape(node_count, capacity), 'node', split_axi...]
    psum x1 -> x0, blocking collectives: 22.1 us -> none  [on_device(): prob_grad = lax.psum(prob_part, 'local').astype(jnp.bfloat16)]
    dot_general x5 -> x0, matrix products: 8.7 us -> none  [the longest x1 1.79 us: on_device(): up_part = jnp.dot(slot_rows, up_weight, preferred_element_type=jnp.float32)]
    all_to_all x2 -> x0, waiting for transfers between devices: 8.12 us -> none  [the longest x1 8.12 us: on_device(): lax.all_to_all(slot_dx.astype(jnp.bfloat16).reshape(node_count, capacity,...]
  transfers between devices with their start and end apart: 7 -> 0, of which waited for: 6 -> 0; matrix products, arithmetic and copies ran while one was open for 3% -> 0% of each run, Pallas kernels for 0% -> 0%
where the time goes in v2:
time: 113 us; the launch traced here: 112 us
  Pallas kernels  110 us (97%)
  local copies, waits for them, and re-layouts  1.89 us (2%)
    pallas_call x1, Pallas kernels, on_device(): pl.pallas_call(functools.partial(moe_kernel, nodes, n), out_shape=(jax.Sh...  110 us

profile of v2, /device:TPU:1, one launch (start us, length us, event | category | flops | bytes accessed | tf_op | source)
XLA Modules:
  0.0 112.4 jit_solution(17490045126300972046)
XLA Ops:
  0.6 109.8 %shard_map.86 = (bf16[32,224]{1,0:T(8,128)(2,1)}, bf16[4,32]{1,0:T(4,128)(2,1)}) custom-call(bf16[32,224]{1,0:T(8,128)(2,1)} %tok_ref.1, bf16[32,224]{1,0:T(8,128)(2,1)} %grad_ref.1, bf16[4,32]{1,0:T(4,128)(2,1)} %bitcast.12, s32[4,32]{1,0:T(4,128)} %bitcast.11, bf16[224,2048]{1,0:T(8,128)(2,1)} %bitcast.8, bf16[224,2048]{1,0:T(8,128)(2,1)} %bitcast.9, ...), custom_call_target="tpu_custom_call" | custom-call | tf_op jit(solution)/shard_map/pallas_call | solution.py:392
  110.5 0.0 copy-start
  110.5 1.3 %copy.11 = bf16[32,224]{1,0:T(8,128)(2,1)} copy(bf16[32,224]{1,0:T(8,128)(2,1)} %get-tuple-element.8) | data formatting | bytes 28672
  111.8 0.0 copy-done
  111.8 0.6 copy.12
Async XLA Ops:
  110.5 1.3 %copy-start = (bf16[4,32]{1,0:T(4,128)(2,1)S(1)}, bf16[4,32]{1,0:T(4,128)(2,1)}, u32[]{:S(2)}) copy-start(bf16[4,32]{1,0:T(4,128)(2,1)} %get-tuple-element.5) | copy-start | bytes 772

commit v3 on v2

--- a/solution.py
+++ b/solution.py
@@ -85,47 +85,49 @@
         return jnp.concatenate([block] * top, axis=0)
 
     held_tokens, held_grads = tok_ref[...].astype(F32), grad_ref[...].astype(F32)
+    first_blocks = jnp.concatenate([held_tokens[:, 0:LANES], held_grads[:, 0:LANES]], axis=1)
+    token_block = jnp.where(
+        lane == rest,
+        prob_col,
+        stacked(jnp.concatenate([held_tokens[:, LANES:columns], blank], axis=1)),
+    )
+    grad_block = stacked(jnp.concatenate([held_grads[:, LANES:columns], blank], axis=1))
     source = jnp.concatenate(
-        [
-            stacked(held_tokens[:, 0:LANES]),
-            jnp.where(
-                lane == rest,
-                prob_col,
-                stacked(jnp.concatenate([held_tokens[:, LANES:columns], blank], axis=1)),
-            ),
-            stacked(held_grads[:, 0:LANES]),
-            stacked(jnp.concatenate([held_grads[:, LANES:columns], blank], axis=1)),
-        ],
-        axis=0,
+        [stacked(first_blocks), jnp.concatenate([token_block, grad_block], axis=1)], axis=0
     ).astype(BF16)
-    target = (expert_row * (4 * CAP) + rank_row).astype(jnp.int32)
-    targets = jnp.concatenate([target + CAP * j for j in range(4)], axis=1)
-    place = ones_where(iota((4 * slots, 4 * pairs), 0) == targets)
-    outbox[...] = mult(place, source).astype(BF16).reshape(outbox.shape)
-    inbox[node] = outbox[node]
+    target = (expert_row * (2 * CAP) + rank_row).astype(jnp.int32)
+    targets = jnp.concatenate([target, target + CAP], axis=1)
+    place = ones_where(iota((2 * slots, 2 * pairs), 0) == targets)
+    filled = mult(place, source)
+    for part in range(2):
+        block = filled[:, part * LANES : (part + 1) * LANES]
+        outbox[part] = block.reshape(outbox.shape[1:]).astype(BF16)
+        inbox[part, node] = outbox[part, node]
 
     pl.semaphore_wait(barrier, nodes + 1)
 
-    def send_copy(peer):
-        return pltpu.make_async_remote_copy(
-            src_ref=outbox.at[peer],
-            dst_ref=inbox.at[node],
-            send_sem=out_send,
-            recv_sem=out_recv,
+    def send_body(part, i):
+        peer = lax.rem(node + i, nodes)
+        pltpu.make_async_remote_copy(
+            src_ref=outbox.at[part, peer],
+            dst_ref=inbox.at[part, node],
+            send_sem=out_send.at[part],
+            recv_sem=out_recv.at[part],
             device_id={"node": peer},
             device_id_type=MESH,
-        )
-
-    def send_body(i, carry):
-        send_copy(lax.rem(node + i, nodes)).start()
-        return carry
-
-    lax.fori_loop(1, nodes, send_body, 0)
-
-    group = 64 // CAP
-    down, along = iota((256, 256), 0), iota((256, 256), 1)
-    sender, rest_of = along // (4 * CAP), along % (4 * CAP)
-    order_in = ones_where(down == 64 * (rest_of // CAP) + CAP * sender + rest_of % CAP)
+        ).start()
+
+    for part in range(2):
+
+        def send_part(i, carry, part=part):
+            send_body(part, i)
+            return carry
+
+        lax.fori_loop(1, nodes, send_part, 0)
+
+    down, along = iota((slots, slots), 0), iota((slots, slots), 1)
+    sender, rest_of = along // (2 * CAP), along % (2 * CAP)
+    order_in = ones_where(down == rows * (rest_of // CAP) + CAP * sender + rest_of % CAP)
     sender2, rest_of2 = down // (2 * CAP), down % (2 * CAP)
     order_out = ones_where(along == rows * (rest_of2 // CAP) + CAP * sender2 + rest_of2 % CAP)
     target2 = (expert_col * (2 * CAP) + rank_col).astype(jnp.int32)
@@ -145,17 +147,21 @@
             device_id_type=MESH,
         )
 
-    all_of(out_send, out_recv, outbox, inbox).wait_recv()
-    arrived = inbox[...].reshape(4 * slots, LANES)
-    blocks = slots // 64
-    mixed = mult(
-        order_in, jnp.concatenate([arrived[256 * g : 256 * g + 256] for g in range(blocks)], axis=1)
-    ).astype(BF16)
-    for g in range(blocks):
-        for j in range(4):
-            xs[64 * g : 64 * g + 64, LANES * j : LANES * (j + 1)] = mixed[
-                64 * j : 64 * j + 64, LANES * g : LANES * (g + 1)
-            ]
+    def all_out(part):
+        return all_of(out_send.at[part], out_recv.at[part], outbox.at[part], inbox.at[part])
+
+    def receive(part):
+        all_out(part).wait_recv()
+        arrived = inbox[part].astype(F32).reshape(2 * slots, LANES).astype(BF16)
+        mixed = mult(
+            order_in, jnp.concatenate([arrived[0:slots], arrived[slots : 2 * slots]], axis=1)
+        ).astype(BF16)
+        for g in range(2):
+            for j in range(2):
+                column = LANES * (2 * part + j)
+                xs[g * rows : (g + 1) * rows, column : column + LANES] = mixed[
+                    j * rows : (j + 1) * rows, g * LANES : (g + 1) * LANES
+                ]
 
     def wrap(c):
         return lax.rem(c + 2 * n, n)
@@ -184,39 +190,44 @@
     def chunks_at(s):
         return (wrap(me + half_ring - s), wrap(me - half_ring + s))
 
-    def terms_for(s):
+    def terms_for(s, kinds):
         for d, c in enumerate(chunks_at(s)):
-            for m in range(3):
+            for m in kinds:
                 terms[d, m] = term(m, c)
 
     longer = ((0, 0), (1, 1))
     shorter = ((0, 1), (1, 0))
 
-    def rs_step(s, fresh):
+    def begin(d, s, h, m, own):
+        start[d, h, m] = own.astype(BF16)
+        rs_copy(d, s, h, m, start.at[d, h, m]).start()
+
+    def go_on(d, s, h, m):
+        held = land.at[d, s - 1, h, m]
+        rs_copy(d, s - 1, h, m, held).wait_recv()
+        held[...] = (terms[d, m, own_rows(h)] + held[...].astype(F32)).astype(BF16)
+        rs_copy(d, s, h, m, held).start()
+
+    for kinds in ((0, 1), (2,)):
+        receive(0 if 0 in kinds else 1)
+        for m in kinds:
+            both = term(m, wrap(me + half_ring))
+            for d, h in longer:
+                begin(d, 0, h, m, both[h * rows : (h + 1) * rows])
+        terms_for(1, kinds)
+        for m in kinds:
+            for d, h in shorter:
+                begin(d, 1, h, m, terms[d, m, own_rows(h)])
+    for m in range(3):
+        for d, h in longer:
+            go_on(d, 1, h, m)
+
+    def rs_body(s, carry):
+        terms_for(s, range(3))
         for h in range(2):
             for m in range(3):
                 for d in range(2):
-                    own = terms[d, m, own_rows(h)]
-                    if (d, h) in fresh:
-                        start[d, h, m] = own.astype(BF16)
-                        rs_copy(d, s, h, m, start.at[d, h, m]).start()
-                    else:
-                        held = land.at[d, s - 1, h, m]
-                        rs_copy(d, s - 1, h, m, held).wait_recv()
-                        held[...] = (own + held[...].astype(F32)).astype(BF16)
-                        rs_copy(d, s, h, m, held).start()
-
-    for m in range(3):
-        both = term(m, wrap(me + half_ring))
-        for d, h in longer:
-            start[d, h, m] = both[h * rows : (h + 1) * rows].astype(BF16)
-            rs_copy(d, 0, h, m, start.at[d, h, m]).start()
-    terms_for(1)
-    rs_step(1, shorter)
-
-    def rs_body(s, carry):
-        terms_for(s)
-        rs_step(s, ())
+                    go_on(d, s, h, m)
         return carry
 
     lax.fori_loop(2, half_ring, rs_body, 0)
@@ -344,24 +355,6 @@
         lax.fori_loop(0, half, back_body, 0)
     inbox2[node] = outbox2[node]
 
-    all_of(back_send, back_recv, outbox2, inbox2).wait_recv()
-    returned = inbox2[...].astype(F32).reshape(2 * slots, LANES).astype(BF16)
-    picked = mult(pick, returned)
-    low_sum, high_sum = picked[0:tokens], picked[pairs : pairs + tokens]
-    for k in range(1, top):
-        low_sum += picked[k * tokens : (k + 1) * tokens]
-        high_sum += picked[pairs + k * tokens : pairs + (k + 1) * tokens]
-    dx_ref[:, 0:LANES] = low_sum.astype(BF16)
-    dx_ref[:, LANES:columns] = high_sum[:, 0:rest].astype(BF16)
-    prob_grad = picked[pairs : 2 * pairs, rest : rest + 1]
-    along_row = jnp.sum(jnp.where(diagonal, prob_grad, 0.0), axis=0, keepdims=True)
-    dp_ref[...] = jnp.concatenate(
-        [along_row[:, k * tokens : (k + 1) * tokens] for k in range(top)], axis=0
-    ).astype(BF16)
-
-    all_of(out_send, out_recv, outbox, inbox).wait_send()
-    all_of(back_send, back_recv, outbox2, inbox2).wait_send()
-
     def drain(s, rs_streams, ag_all):
         for d, h in rs_streams:
             for m in range(3):
@@ -379,6 +372,25 @@
 
     lax.fori_loop(1, half_ring - 1, drain_body, 0)
     drain(half_ring - 1, longer + shorter, False)
+    for part in range(2):
+        all_out(part).wait_send()
+
+    all_of(back_send, back_recv, outbox2, inbox2).wait_recv()
+    returned = inbox2[...].astype(F32).reshape(2 * slots, LANES).astype(BF16)
+    picked = mult(pick, returned)
+    low_sum, high_sum = picked[0:tokens], picked[pairs : pairs + tokens]
+    for k in range(1, top):
+        low_sum += picked[k * tokens : (k + 1) * tokens]
+        high_sum += picked[pairs + k * tokens : pairs + (k + 1) * tokens]
+    dx_ref[:, 0:LANES] = low_sum
+    dx_ref[:, LANES:columns] = high_sum[:, 0:rest]
+    prob_grad = picked[pairs : 2 * pairs, rest : rest + 1]
+    along_row = jnp.sum(jnp.where(diagonal, prob_grad, 0.0), axis=0, keepdims=True)
+    dp_ref[...] = jnp.concatenate(
+        [along_row[:, k * tokens : (k + 1) * tokens] for k in range(top)], axis=0
+    )
+
+    all_of(back_send, back_recv, outbox2, inbox2).wait_send()
 
 
 def on_device(tokens, grad_out, route_prob, route_expert, w_gate, w_up, w_down):
@@ -392,8 +404,8 @@
     grad_tokens, grad_prob = pl.pallas_call(
         functools.partial(moe_kernel, nodes, n),
         out_shape=(
-            jax.ShapeDtypeStruct(tokens.shape, BF16),
-            jax.ShapeDtypeStruct((top, block_tokens), BF16),
+            jax.ShapeDtypeStruct(tokens.shape, F32),
+            jax.ShapeDtypeStruct((top, block_tokens), F32),
         ),
         in_specs=[vmem] * 4 + [hbm] * 3,
         out_specs=(vmem, vmem),
@@ -401,8 +413,8 @@
             pltpu.VMEM((width, hidden), BF16),
             pltpu.VMEM((width, hidden), BF16),
             pltpu.VMEM((width, hidden), BF16),
-            pltpu.VMEM((nodes, 4 * CAP, LANES), BF16),
-            pltpu.VMEM((nodes, 4 * CAP, LANES), BF16),
+            pltpu.VMEM((2, nodes, 2 * CAP, LANES), BF16),
+            pltpu.VMEM((2, nodes, 2 * CAP, LANES), BF16),
             pltpu.VMEM((slots, 4 * LANES), BF16),
             pltpu.VMEM((2, 3, slots, chunk), F32),
             pltpu.VMEM((2, 2, 3, rows, chunk), BF16),
@@ -413,8 +425,8 @@
             pltpu.VMEM((nodes, 2 * CAP, LANES), BF16),
             pltpu.VMEM((nodes, 2 * CAP, LANES), BF16),
             dma((3,)),
-            dma,
-            dma,
+            dma((2,)),
+            dma((2,)),
             dma((2, half_ring, 2, 3)),
             dma((2, half_ring, 2, 3)),
             dma((2, half_ring, 5)),
@@ -434,7 +446,7 @@
         w_up[0],
         jnp.swapaxes(w_down[0], 0, 1),
     )
-    return grad_tokens, grad_prob.T
+    return grad_tokens.astype(BF16), grad_prob.T.astype(BF16)
 
 
 def solution(mesh):

time: 113 us -> 110 us (0.973)
  Pallas kernels: 110 us -> 107 us
  other arithmetic: 0 us -> 1.93 us
  local copies, waits for them, and re-layouts: 1.89 us -> 0.01 us
    pallas_call x1, Pallas kernels: 110 us -> 107 us  [on_device(): pl.pallas_call(functools.partial(moe_kernel, nodes, n), out_shape=(jax.Sh...]
    convert_element_type x0 -> x2, other arithmetic: none -> 1.93 us  [on_device(): return (grad_tokens.astype(BF16), grad_prob.T.astype(BF16))]
    unnamed x4 -> x2, local copies, waits for them, and re-layouts: 1.89 us -> 0.01 us
where the time goes in v3:
time: 110 us
  Pallas kernels  107 us (97%)
  other arithmetic  1.93 us (2%)
    pallas_call x1, Pallas kernels, on_device(): pl.pallas_call(functools.partial(moe_kernel, nodes, n), out_shape=(jax.Sh...  107 us

profile of v3, /device:TPU:1, one launch (start us, length us, event | category | flops | bytes accessed | tf_op | source)
XLA Modules:
  0.0 109.9 jit_solution(16816711381455187241)
XLA Ops:
  0.6 107.3 %shard_map.86 = (f32[32,224]{1,0:T(8,128)}, f32[4,32]{1,0:T(4,128)}) custom-call(bf16[32,224]{1,0:T(8,128)(2,1)} %tok_ref.1, bf16[32,224]{1,0:T(8,128)(2,1)} %grad_ref.1, bf16[4,32]{1,0:T(4,128)(2,1)} %bitcast.13, s32[4,32]{1,0:T(4,128)} %bitcast.12, bf16[224,2048]{1,0:T(8,128)(2,1)} %bitcast.9, bf16[224,2048]{1,0:T(8,128)(2,1)} %bitcast.10, ...), custom_call_target="tpu_custom_call" | custom-call | tf_op jit(solution)/shard_map/pallas_call | solution.py:404
  107.9 0.0 copy-start
  107.9 1.4 %convert_element_type.9 = bf16[32,224]{1,0:T(8,128)(2,1)} convert(f32[32,224]{1,0:T(8,128)} %get-tuple-element.4) | non-fusion elementwise | flops 7168 | bytes 43008 | tf_op jit(solution)/shard_map/convert_element_type | solution.py:449
  109.3 0.0 copy-done
  109.3 0.6 convert_bitcast_fusion
Async XLA Ops:
  107.9 1.4 %copy-start = (f32[4,32]{1,0:T(4,128)S(1)}, f32[4,32]{1,0:T(4,128)}, u32[]{:S(2)}) copy-start(f32[4,32]{1,0:T(4,128)} %get-tuple-element.5) | copy-start | bytes 1540

commit v4 on v3

--- a/solution.py
+++ b/solution.py
@@ -106,8 +106,11 @@
 
     pl.semaphore_wait(barrier, nodes + 1)
 
+    def beside(i):
+        return (1 - 2 * lax.rem(i, 2)) * ((i + 1) // 2)
+
     def send_body(part, i):
-        peer = lax.rem(node + i, nodes)
+        peer = lax.rem(node + beside(i) + nodes, nodes)
         pltpu.make_async_remote_copy(
             src_ref=outbox.at[part, peer],
             dst_ref=inbox.at[part, node],
@@ -234,7 +237,7 @@
     for m in range(3):
         terms[0, m] = term(m, me)
 
-    order = (0, 1, 4, 2, 3)
+    order = (0, 1, 2, 4, 3)
 
     def is_longer(d, q):
         return d == (0 if q < 2 else 1)
@@ -263,36 +266,40 @@
         )
 
     last = half_ring - 1
-    for h in range(2):
+    ones = jnp.ones((8, chunk), BF16)
+    whole = []
+    for q in range(4):
+        h, own = q // 2, slice((q % 2) * piece, (q % 2 + 1) * piece)
         sums = []
         for m in range(3):
-            total = terms[0, m, own_rows(h)]
+            total = terms[0, m, pl.ds(q * piece, piece)]
             for d in range(2):
-                rs_copy(d, last, h, m, land.at[d, last, h, m]).wait_recv()
-                total = total + land[d, last, h, m].astype(F32)
+                if q % 2 == 0:
+                    rs_copy(d, last, h, m, land.at[d, last, h, m]).wait_recv()
+                total = total + land[d, last, h, m, own].astype(F32)
             sums.append(total)
         gate, up, back = sums
-        prob = xs[own_rows(h), columns : columns + 1].astype(F32)
+        prob = xs[pl.ds(q * piece, piece), columns : columns + 1].astype(F32)
         squash = jax.nn.sigmoid(gate)
         gated = gate * squash
         hidden = back * prob
-        ag[me, own_rows(h), 0:chunk] = (
-            hidden * up * squash * (1.0 + gate * (1.0 - squash))
+        grad_gate = hidden * up * squash * (1.0 + gate * (1.0 - squash))
+        ag[me, pl.ds(q * piece, piece)] = jnp.concatenate(
+            [grad_gate, hidden * gated], axis=1
         ).astype(BF16)
-        ag[me, own_rows(h), chunk : 2 * chunk] = (hidden * gated).astype(BF16)
-        if h == 0:
-            for q in (0, 1):
-                for d in range(2):
-                    ag_copy(d, 0, q, me).start()
-        both = gated * up * back
-        high = both.astype(BF16)
-        low = (both - high.astype(F32)).astype(BF16)
-        ones = jnp.ones((8, chunk), BF16)
-        part = lax.dot_general(ones, high, CROSS, preferred_element_type=F32) + lax.dot_general(
-            ones, low, CROSS, preferred_element_type=F32
-        )
-        pp[me, 4 * h : 4 * h + 4] = part[0:4]
-    for q in (4, 2, 3):
+        whole.append(gated * up * back)
+        if q < 3:
+            for d in range(2):
+                ag_copy(d, 0, q, me).start()
+        if q % 2 == 1:
+            both = jnp.concatenate(whole[q - 1 :], axis=0)
+            high = both.astype(BF16)
+            low = (both - high.astype(F32)).astype(BF16)
+            part = lax.dot_general(ones, high, CROSS, preferred_element_type=F32) + lax.dot_general(
+                ones, low, CROSS, preferred_element_type=F32
+            )
+            pp[me, 4 * h : 4 * h + 4] = part[0:4]
+    for q in (4, 3):
         for d in range(2):
             ag_copy(d, 0, q, me).start()
     acc[...] = product(me, 0, slots)
@@ -344,7 +351,7 @@
         )
 
         def back_body(i, carry, h=h, half=half):
-            peer = h * half + lax.rem(node + i, half)
+            peer = h * half + lax.rem(node + beside(i) + nodes, half)
 
             @pl.when(peer != node)
             def _():

time: 110 us -> 109 us (level)
  no operation moved by 1% of the time
where the time goes in v4:
time: 109 us
  Pallas kernels  106 us (97%)
  other arithmetic  1.93 us (2%)
    pallas_call x1, Pallas kernels, on_device(): pl.pallas_call(functools.partial(moe_kernel, nodes, n), out_shape=(jax.Sh...  106 us

profile of v4, /device:TPU:1, one launch (start us, length us, event | category | flops | bytes accessed | tf_op | source)
XLA Modules:
  0.0 109.0 jit_solution(2927415862491723838)
XLA Ops:
  0.6 106.4 %shard_map.86 = (f32[32,224]{1,0:T(8,128)}, f32[4,32]{1,0:T(4,128)}) custom-call(bf16[32,224]{1,0:T(8,128)(2,1)} %tok_ref.1, bf16[32,224]{1,0:T(8,128)(2,1)} %grad_ref.1, bf16[4,32]{1,0:T(4,128)(2,1)} %bitcast.13, s32[4,32]{1,0:T(4,128)} %bitcast.12, bf16[224,2048]{1,0:T(8,128)(2,1)} %bitcast.9, bf16[224,2048]{1,0:T(8,128)(2,1)} %bitcast.10, ...), custom_call_target="tpu_custom_call" | custom-call | tf_op jit(solution)/shard_map/pallas_call | solution.py:411
  107.0 0.0 copy-start
  107.0 1.4 %convert_element_type.9 = bf16[32,224]{1,0:T(8,128)(2,1)} convert(f32[32,224]{1,0:T(8,128)} %get-tuple-element.4) | non-fusion elementwise | flops 7168 | bytes 43008 | tf_op jit(solution)/shard_map/convert_element_type | solution.py:456
  108.4 0.0 copy-done
  108.4 0.6 convert_bitcast_fusion
Async XLA Ops:
  107.0 1.4 %copy-start = (f32[4,32]{1,0:T(4,128)S(1)}, f32[4,32]{1,0:T(4,128)}, u32[]{:S(2)}) copy-start(f32[4,32]{1,0:T(4,128)} %get-tuple-element.5) | copy-start | bytes 1540
